TPU v7x, 32 devices: a whole 2x2x4 slice. The times are simulated.
32 devices in a mesh: grp: 2 (over y), space: 4 (over z), seg: 2 (over x), var: 2 (over core).
Axes of the slice: x: 2, y: 2, z: 4, core: 2. Of those that a mesh axis runs over, the one named last changes fastest.
Arguments:
- snapshots: bfloat16 [1024, 5, 2048], P(('grp', 'seg'), None, 'space'), parts along dimension 0, may hold values from -6 to 6
- weights: float32 [5, 4096], P(None, ('grp', 'space')), parts along dimension 1, may hold values from 0.4 to 10, as said below
- bins: int32 [32], replicated, may hold values from 1 to 127, as said below
Outputs:
- modes: float32 [32, 6, 5, 4096], P(('seg', 'var'), None, None, ('grp', 'space')), parts along dimension 3
- factor: float32 [64, 6, 6], P(('grp', 'seg', 'var')), parts along dimension 0
There are 2 independent parts, one for each index of `grp`. A program takes and returns all parts, laid end to end along the dimension named above; an argument that names none is the same for every part. Nothing has to cross between parts.
Inputs may be any that keep to these rules, and one draw needn't show every extreme that they name: Positive quadrature weights. bins lie strictly between the zero bin and the Nyquist bin of a block.
All inputs are finite; a program needn't handle non-finite values.
Results may differ from a plain program's by a relative error of at most 0.0042.
Values may be sent and summed in bfloat16 or wider, within the bound.
A program may use at most 64 MiB of HBM per device.

v0:
```python
import functools
import math

import jax
import jax.numpy as jnp
from jax import lax
from jax.experimental import pallas as pl
from jax.experimental.pallas import tpu as pltpu
from jax.sharding import PartitionSpec as P


def window_basis(offset, bin_index, length):
    phase = offset * bin_index % length
    angle = 2.0 * math.pi / length * phase.astype(jnp.float32)
    taper = 0.5 - 0.5 * jnp.cos(2.0 * math.pi / length * offset.astype(jnp.float32))
    factor = taper / math.sqrt(0.375 * length)
    return (factor * jnp.cos(angle), -factor * jnp.sin(angle))


def invert_lower(lower):
    identity = jnp.eye(lower.shape[-1], dtype=lower.dtype)

    def solve_single(single):
        return jax.scipy.linalg.solve_triangular(single, identity, lower=True)

    return jax.vmap(solve_single)(lower)


MESH = pl.DeviceIdType.MESH


def cosine_of(phase, length):
    quarter = jnp.abs(phase - length // 2) - length // 4
    x = quarter.astype(jnp.float32) * (2.0 * math.pi / length)
    y = x * x
    poly = -1.0 / 39916800.0
    for term in (1.0 / 362880.0, -1.0 / 5040.0, 1.0 / 120.0, -1.0 / 6.0, 1.0):
        poly = poly * y + term
    return x * poly


def basis_rows(bins_ref, frames, seg, var, var_count):
    freq = 8
    shape = (freq, frames)
    frame = lax.broadcasted_iota(jnp.int32, shape, 1)
    row = lax.broadcasted_iota(jnp.int32, shape, 0)
    half = frames // 2
    taper = (0.5 - 0.5 * cosine_of(frame, frames)) / math.sqrt(0.375 * frames)
    second = (lax.broadcasted_iota(jnp.int32, (2 * freq, frames), 1) >= half).astype(jnp.int32)
    overlap = second == 1 - seg
    rows = []
    for group in range(2):
        owner = 1 - seg if group == 0 else seg
        first = (owner * var_count + var) * freq
        bin_of = jnp.zeros(shape, jnp.int32)
        for f in range(freq):
            bin_of = jnp.where(row == f, bins_ref[first + f], bin_of)
        phase = (frame * bin_of) & (frames - 1)
        cosine = taper * cosine_of(phase, frames)
        sine = taper * cosine_of((phase + frames // 4) & (frames - 1), frames)
        whole = jnp.concatenate([cosine, sine], 0)
        shared = jnp.concatenate([whole[:, half:], whole[:, :half]], 1)
        rows += [whole, jnp.where(overlap, shared, 0.0)]
    return jnp.concatenate(rows, 0).astype(jnp.bfloat16)


def kernel(space_count, var_count, x_hbm, w_hbm, bins_hbm, values, gram_ref,
           x_vmem, w_ref, bins_ref, own_half, send, recv, gram_buf,
           x_sem, w_sem, bins_sem, send_sem, recv_sem, g_send_sem, g_recv_sem):
    variables, frames, cells = x_hbm.shape
    freq = 8
    rows = 2 * freq
    seg = lax.axis_index("seg")
    var = lax.axis_index("var")
    me = lax.axis_index("space")
    other = 1 - seg
    bins_load = pltpu.make_async_copy(bins_hbm, bins_ref, bins_sem)
    bins_load.start()
    loads = []
    for v in range(variables):
        load = pltpu.make_async_copy(x_hbm.at[v], x_vmem.at[v], x_sem.at[v])
        load.start()
        loads.append(load)

    w_load = pltpu.make_async_copy(w_hbm, w_ref, w_sem)
    w_load.start()

    barrier = pltpu.get_barrier_semaphore()
    pl.semaphore_signal(barrier, inc=1, device_id={"seg": other}, device_id_type=MESH)
    for d in range(1, space_count):
        pl.semaphore_signal(
            barrier, inc=1, device_id={"space": lax.rem(me + d, space_count)}, device_id_type=MESH)

    bins_load.wait()
    basis = basis_rows(bins_ref, frames, seg, var, var_count)

    pl.semaphore_wait(barrier, space_count)
    copies = [
        pltpu.make_async_remote_copy(
            src_ref=send.at[v], dst_ref=recv.at[v], send_sem=send_sem.at[v], recv_sem=recv_sem.at[v],
            device_id={"seg": other}, device_id_type=MESH)
        for v in range(variables)]

    def transform(v):
        loads[v].wait()
        summed = jnp.dot(basis, x_vmem[v], preferred_element_type=jnp.float32)
        send[v] = summed[:2 * rows].astype(send.dtype)
        own = summed[2 * rows:3 * rows].astype(jnp.bfloat16).astype(jnp.float32)
        own_half[v] = summed[3 * rows:]
        for part in range(2):
            values[3 * part + 2 * seg, v] = own[part * freq:(part + 1) * freq]

    @pl.when(var == 0)
    def _():
        for v in range(variables):
            transform(v)
            copies[v].start()

    @pl.when(var != 0)
    def _():
        for v in range(variables):
            transform(v)
        for copy in copies:
            copy.start()

    w_load.wait()
    columns = 6
    pairs = [(i, j) for i in range(columns) for j in range(i + 1)]
    sums = [None] * len(pairs)
    for v in range(variables):
        copies[v].wait_recv()
        far = recv[v].astype(jnp.float32)
        total = own_half[v] + far[rows:]
        total = total.astype(jnp.bfloat16).astype(jnp.float32)
        for part in range(2):
            values[3 * part + 1, v] = total[part * freq:(part + 1) * freq]
            values[3 * part + 2 * other, v] = far[part * freq:(part + 1) * freq]
        for at in range(0, cells, 128):
            one = pl.ds(at, 128)
            weight = jnp.broadcast_to(w_ref[v:v + 1, one], (freq, 128))
            plain = [values[i, v, :, one] for i in range(columns)]
            scaled = [p * weight for p in plain]
            for n, (i, j) in enumerate(pairs):
                term = scaled[i] * plain[j]
                sums[n] = term if sums[n] is None else sums[n] + term

    lane = lax.broadcasted_iota(jnp.int32, (freq, 128), 1)
    packed = jnp.zeros((freq, 128), jnp.float32)
    for n in range(len(pairs)):
        packed = jnp.where(lane == n, jnp.sum(sums[n], axis=1, keepdims=True), packed)
    gram_buf[me] = packed
    g_copies = []
    for d in range(1, space_count):
        copy = pltpu.make_async_remote_copy(
            src_ref=gram_buf.at[me], dst_ref=gram_buf.at[me],
            send_sem=g_send_sem.at[d - 1], recv_sem=g_recv_sem.at[d - 1],
            device_id={"space": lax.rem(me + d, space_count)}, device_id_type=MESH)
        copy.start()
        g_copies.append(copy)
    for copy in g_copies:
        copy.wait_recv()
    gram = gram_buf[0]
    for d in range(1, space_count):
        gram = gram + gram_buf[d]
    gram_ref[...] = gram

    for copy in copies + g_copies:
        copy.wait_send()


def modes_kernel(space_count, values, gram_ref, modes_hbm, factor_hbm, modes_vmem, factor_ref, modes_sem, factor_sem):
    columns, variables, freq, cells = values.shape
    pairs = [(i, j) for i in range(columns) for j in range(i + 1)]
    lane = lax.broadcasted_iota(jnp.int32, (freq, 128), 1)
    gram = gram_ref[...] * (1.0 / (variables * cells * space_count))
    entry = {
        pair: jnp.broadcast_to(gram[:, n:n + 1], (freq, 128)) for n, pair in enumerate(pairs)}

    lower, inverse = {}, {}
    for j in range(columns):
        rest = entry[j, j]
        for k in range(j):
            rest = rest - lower[j, k] * lower[j, k]
        inverse[j, j] = lax.rsqrt(rest)
        lower[j, j] = rest * inverse[j, j]
        for i in range(j + 1, columns):
            rest = entry[i, j]
            for k in range(j):
                rest = rest - lower[i, k] * lower[j, k]
            lower[i, j] = rest * inverse[j, j]
    for j in range(columns):
        for i in range(j + 1, columns):
            total = lower[i, j] * inverse[j, j]
            for k in range(j + 1, i):
                total = total + lower[i, k] * inverse[k, j]
            inverse[i, j] = -total * inverse[i, i]

    for i in range(columns):
        line = jnp.zeros((freq, 128), jnp.float32)
        for j in range(i, columns):
            line = jnp.where(lane == j, lower[j, i], line)
        factor_ref[i] = line[:, :columns]

    copies = [pltpu.make_async_copy(factor_ref, factor_hbm, factor_sem)]
    copies[0].start()
    for i in range(columns):
        for v in range(variables):
            for at in range(0, cells, 128):
                one = pl.ds(at, 128)
                mode = inverse[i, 0] * values[0, v, :, one]
                for j in range(1, i + 1):
                    mode = mode + inverse[i, j] * values[j, v, :, one]
                modes_vmem[i, v, :, one] = mode
        copy = pltpu.make_async_copy(modes_vmem.at[i], modes_hbm.at[i], modes_sem.at[i])
        copy.start()
        copies.append(copy)
    for copy in copies:
        copy.wait()


def on_device_kernel(snapshots, weights, bins):
    frames, variables, cells = snapshots.shape
    space_count = lax.axis_size("space")
    freq, columns = 8, 6
    rows = 2 * freq
    dma = pltpu.SemaphoreType.DMA
    inputs = [jnp.transpose(snapshots, (1, 0, 2)), weights, bins]
    inputs = [pltpu.with_memory_space_constraint(value, pltpu.HBM) for value in inputs]
    values, gram = pl.pallas_call(
        functools.partial(kernel, space_count, lax.axis_size("var")),
        out_shape=(
            jax.ShapeDtypeStruct((columns, variables, freq, cells), jnp.float32),
            jax.ShapeDtypeStruct((freq, 128), jnp.float32),
        ),
        in_specs=[
            pl.BlockSpec(memory_space=pltpu.HBM),
            pl.BlockSpec(memory_space=pltpu.HBM),
            pl.BlockSpec(memory_space=pltpu.HBM),
        ],
        out_specs=(pl.BlockSpec(memory_space=pltpu.VMEM),) * 2,
        scratch_shapes=[
            pltpu.VMEM((variables, frames, cells), jnp.bfloat16),
            pltpu.VMEM((variables, cells), jnp.float32),
            pltpu.SMEM(bins.shape, jnp.int32),
            pltpu.VMEM((variables, rows, cells), jnp.float32),
            pltpu.VMEM((variables, 2 * rows, cells), jnp.bfloat16),
            pltpu.VMEM((variables, 2 * rows, cells), jnp.bfloat16),
            pltpu.VMEM((space_count, freq, 128), jnp.float32),
            dma((variables,)), dma, dma,
            dma((variables,)), dma((variables,)),
            dma((space_count - 1,)), dma((space_count - 1,)),
        ],
        compiler_params=pltpu.CompilerParams(
            collective_id=0, has_side_effects=True, vmem_limit_bytes=32 * 1024 * 1024),
    )(*inputs)
    modes, factor = pl.pallas_call(
        functools.partial(modes_kernel, space_count),
        out_shape=(
            jax.ShapeDtypeStruct((columns, variables, freq, cells), jnp.float32),
            jax.ShapeDtypeStruct((columns, freq, columns), jnp.float32),
        ),
        in_specs=[pl.BlockSpec(memory_space=pltpu.VMEM)] * 2,
        out_specs=(pl.BlockSpec(memory_space=pltpu.HBM),) * 2,
        scratch_shapes=[
            pltpu.VMEM((columns, variables, freq, cells), jnp.float32),
            pltpu.VMEM((columns, freq, columns), jnp.float32),
            dma((columns,)), dma,
        ],
        compiler_params=pltpu.CompilerParams(vmem_limit_bytes=16 * 1024 * 1024),
    )(values, gram)
    return jnp.transpose(modes, (2, 0, 1, 3)), jnp.transpose(factor, (1, 0, 2))


def on_device(snapshots, weights, bins):
    seg_count = lax.axis_size("seg")
    var_count = lax.axis_size("var")
    space_count = lax.axis_size("space")
    frames, variables, cell_dev = snapshots.shape
    flat_rows = variables * cell_dev
    hop_len = frames // 2
    block_count = 2 * seg_count - 1
    freq_dev = bins.shape[0] // (seg_count * var_count)
    own = snapshots.reshape(frames, flat_rows)
    start_bin = (lax.axis_index("seg") * var_count + lax.axis_index("var")) * freq_dev
    chosen = lax.dynamic_slice_in_dim(bins, start_bin, freq_dev)
    piece = lax.all_gather(own, "seg", axis=0, tiled=True)
    count = piece.shape[0]
    moments = jnp.arange(count, dtype=jnp.int32)
    offset = moments[:, None] - hop_len * jnp.arange(block_count, dtype=jnp.int32)[None, :]
    inside = (offset >= 0) & (offset < frames)
    safe_offset = jnp.where(inside, offset, 0)
    cosine, sine = window_basis(safe_offset[:, :, None], chosen[None, None, :], frames)
    coeffs = jnp.stack([cosine, sine], 3) * inside[:, :, None, None].astype(jnp.float32)
    coeffs = jnp.transpose(coeffs, (0, 2, 3, 1)).reshape(count, freq_dev * 2 * block_count)
    coeffs = coeffs.astype(jnp.bfloat16)
    summed = jnp.einsum("pk,pr->kr", coeffs, piece, preferred_element_type=jnp.float32)
    spectra = summed.astype(jnp.bfloat16).reshape(freq_dev, 2 * block_count, flat_rows)
    values = spectra.astype(jnp.float32)
    scaled = values * weights.reshape(flat_rows)
    local_gram = jnp.einsum("fir,fjr->fij", scaled, values, precision=lax.Precision.HIGHEST)
    local_gram = local_gram / (variables * cell_dev * space_count)
    lower = jnp.linalg.cholesky(lax.psum(local_gram, "space"))
    inverse = invert_lower(lower)
    modes = jnp.einsum("fij,fjr->fir", inverse, values, precision=lax.Precision.HIGHEST)
    modes = modes.reshape(freq_dev, 2 * block_count, variables, cell_dev)
    return (modes, jnp.swapaxes(lower, 1, 2))


def per_device(snapshots, weights, bins):
    seg_count = lax.axis_size("seg")
    frames, variables, cells = snapshots.shape
    freq_dev = bins.shape[0] // (seg_count * lax.axis_size("var"))
    fits = seg_count == 2 and lax.axis_size("var") == 2 and freq_dev == 8 and cells % 128 == 0
    fits = fits and frames >= 256 and frames & (frames - 1) == 0 and lax.axis_size("space") > 1
    return (on_device_kernel if fits else on_device)(snapshots, weights, bins)


def solution(mesh):
    return jax.shard_map(
        per_device,
        mesh=mesh,
        in_specs=(P(("grp", "seg"), None, "space"), P(None, ("grp", "space")), P()),
        out_specs=(
            P(("seg", "var"), None, None, ("grp", "space")),
            P(("grp", "seg", "var"), None, None),
        ),
        check_vma=False,
    )
```

profile of v0, /device:TPU:0, one launch (start us, length us, event | category | flops | bytes accessed | tf_op | source)
XLA Modules:
  0.0 16.0 jit_solution(15804798433602874780)
XLA Ops:
  0.6 14.4 %shard_map.50 = (f32[6,5,8,512]{3,2,1,0:T(8,128)S(1)}, f32[8,128]{1,0:T(8,128)S(1)}) custom-call(bf16[5,256,512]{2,1,0:T(8,128)(2,1)} %bitcast.3, f32[5,512]{1,0:T(8,128)} %w_hbm.1, s32[32]{0:T(128)} %bins_hbm.1), custom_call_target="tpu_custom_call" | custom-call | tf_op jit(solution)/shard_map/pallas_call | solution.py:229
  15.1 0.9 %shard_map.51 = (f32[6,5,8,512]{3,2,1,0:T(8,128)}, f32[6,8,6]{2,1,0:T(8,128)}) custom-call(f32[6,5,8,512]{3,2,1,0:T(8,128)S(1)} %get-tuple-element.6.values, f32[8,128]{1,0:T(8,128)S(1)} %get-tuple-element.7.gram_ref), custom_call_target="tpu_custom_call" | custom-call | tf_op jit(solution)/shard_map/pallas_call | solution.py:256
where the time goes:
time: 16.2 us; the launch traced here: 16 us
  Pallas kernels  15.4 us (95%)
  between operations  0.64 us (4%)
    pallas_call x1, Pallas kernels, on_device_kernel(): pl.pallas_call(functools.partial(kernel, space_count, lax.axis_size('var'...  14.4 us
    pallas_call x1, Pallas kernels, on_device_kernel(): pl.pallas_call(functools.partial(modes_kernel, space_count), out_shape=(j...  0.92 us

commit v1 on v0

--- a/solution.py
+++ b/solution.py
@@ -66,7 +66,7 @@
 
 def kernel(space_count, var_count, x_hbm, w_hbm, bins_hbm, values, gram_ref,
            x_vmem, w_ref, bins_ref, own_half, send, recv, gram_buf,
-           x_sem, w_sem, bins_sem, send_sem, recv_sem, g_send_sem, g_recv_sem):
+           x_sem, w_sem, bins_sem, send_sem, recv_sem, g_send_sem, g_recv_sem, turn_sem):
     variables, frames, cells = x_hbm.shape
     freq = 8
     rows = 2 * freq
@@ -87,6 +87,7 @@
 
     barrier = pltpu.get_barrier_semaphore()
     pl.semaphore_signal(barrier, inc=1, device_id={"seg": other}, device_id_type=MESH)
+    pl.semaphore_signal(barrier, inc=1, device_id={"var": 1 - var}, device_id_type=MESH)
     for d in range(1, space_count):
         pl.semaphore_signal(
             barrier, inc=1, device_id={"space": lax.rem(me + d, space_count)}, device_id_type=MESH)
@@ -94,7 +95,8 @@
     bins_load.wait()
     basis = basis_rows(bins_ref, frames, seg, var, var_count)
 
-    pl.semaphore_wait(barrier, space_count)
+    pl.semaphore_wait(barrier, space_count + 1)
+    early = 2
     copies = [
         pltpu.make_async_remote_copy(
             src_ref=send.at[v], dst_ref=recv.at[v], send_sem=send_sem.at[v], recv_sem=recv_sem.at[v],
@@ -115,11 +117,15 @@
         for v in range(variables):
             transform(v)
             copies[v].start()
+        for copy in copies[:early]:
+            copy.wait_send()
+        pl.semaphore_signal(turn_sem, inc=1, device_id={"var": 1 - var}, device_id_type=MESH)
 
     @pl.when(var != 0)
     def _():
         for v in range(variables):
             transform(v)
+        pl.semaphore_wait(turn_sem, 1)
         for copy in copies:
             copy.start()
 
@@ -164,7 +170,12 @@
         gram = gram + gram_buf[d]
     gram_ref[...] = gram
 
-    for copy in copies + g_copies:
+    @pl.when(var != 0)
+    def _():
+        for copy in copies[:early]:
+            copy.wait_send()
+
+    for copy in copies[early:] + g_copies:
         copy.wait_send()
 
 
@@ -249,6 +260,7 @@
             dma((variables,)), dma, dma,
             dma((variables,)), dma((variables,)),
             dma((space_count - 1,)), dma((space_count - 1,)),
+            pltpu.SemaphoreType.REGULAR,
         ],
         compiler_params=pltpu.CompilerParams(
             collective_id=0, has_side_effects=True, vmem_limit_bytes=32 * 1024 * 1024),

time: 16.2 us -> 14.8 us (0.914)
  the two profiles are of different devices: /device:TPU:0 before, /device:TPU:1 now
where the time goes in v1:
time: 14.8 us; the launch traced here: 14.7 us
  Pallas kernels  14.1 us (95%)
  between operations  0.64 us (4%)
    pallas_call x1, Pallas kernels, on_device_kernel(): pl.pallas_call(functools.partial(kernel, space_count, lax.axis_size('var'...  13.1 us
    pallas_call x1, Pallas kernels, on_device_kernel(): pl.pallas_call(functools.partial(modes_kernel, space_count), out_shape=(j...  0.92 us

profile of v1, /device:TPU:1, one launch (start us, length us, event | category | flops | bytes accessed | tf_op | source)
XLA Modules:
  0.0 14.7 jit_solution(10414735718050568952)
XLA Ops:
  0.6 13.1 %shard_map.50 = (f32[6,5,8,512]{3,2,1,0:T(8,128)S(1)}, f32[8,128]{1,0:T(8,128)S(1)}) custom-call(bf16[5,256,512]{2,1,0:T(8,128)(2,1)} %bitcast.3, f32[5,512]{1,0:T(8,128)} %w_hbm.1, s32[32]{0:T(128)} %bins_hbm.1), custom_call_target="tpu_custom_call" | custom-call | tf_op jit(solution)/shard_map/pallas_call | solution.py:240
  13.8 0.9 %shard_map.51 = (f32[6,5,8,512]{3,2,1,0:T(8,128)}, f32[6,8,6]{2,1,0:T(8,128)}) custom-call(f32[6,5,8,512]{3,2,1,0:T(8,128)S(1)} %get-tuple-element.6.values, f32[8,128]{1,0:T(8,128)S(1)} %get-tuple-element.7.gram_ref), custom_call_target="tpu_custom_call" | custom-call | tf_op jit(solution)/shard_map/pallas_call | solution.py:268

commit v2 on v1

--- a/solution.py
+++ b/solution.py
@@ -76,11 +76,8 @@
     other = 1 - seg
     bins_load = pltpu.make_async_copy(bins_hbm, bins_ref, bins_sem)
     bins_load.start()
-    loads = []
     for v in range(variables):
-        load = pltpu.make_async_copy(x_hbm.at[v], x_vmem.at[v], x_sem.at[v])
-        load.start()
-        loads.append(load)
+        pltpu.make_async_copy(x_hbm.at[v], x_vmem.at[v], x_sem.at[v]).start()
 
     w_load = pltpu.make_async_copy(w_hbm, w_ref, w_sem)
     w_load.start()
@@ -104,7 +101,7 @@
         for v in range(variables)]
 
     def transform(v):
-        loads[v].wait()
+        pltpu.make_async_copy(x_hbm.at[v], x_vmem.at[v], x_sem.at[v]).wait()
         summed = jnp.dot(basis, x_vmem[v], preferred_element_type=jnp.float32)
         send[v] = summed[:2 * rows].astype(send.dtype)
         own = summed[2 * rows:3 * rows].astype(jnp.bfloat16).astype(jnp.float32)
@@ -123,8 +120,7 @@
 
     @pl.when(var != 0)
     def _():
-        for v in range(variables):
-            transform(v)
+        pl.loop(0, variables)(transform)
         pl.semaphore_wait(turn_sem, 1)
         for copy in copies:
             copy.start()
@@ -132,7 +128,7 @@
     w_load.wait()
     columns = 6
     pairs = [(i, j) for i in range(columns) for j in range(i + 1)]
-    sums = [None] * len(pairs)
+    sums = tuple(jnp.zeros((freq, 128), jnp.float32) for _ in pairs)
     for v in range(variables):
         copies[v].wait_recv()
         far = recv[v].astype(jnp.float32)
@@ -141,14 +137,15 @@
         for part in range(2):
             values[3 * part + 1, v] = total[part * freq:(part + 1) * freq]
             values[3 * part + 2 * other, v] = far[part * freq:(part + 1) * freq]
-        for at in range(0, cells, 128):
-            one = pl.ds(at, 128)
+        def add_block(block, sums, v=v):
+            one = pl.ds(pl.multiple_of(block * 128, 128), 128)
             weight = jnp.broadcast_to(w_ref[v:v + 1, one], (freq, 128))
             plain = [values[i, v, :, one] for i in range(columns)]
             scaled = [p * weight for p in plain]
-            for n, (i, j) in enumerate(pairs):
-                term = scaled[i] * plain[j]
-                sums[n] = term if sums[n] is None else sums[n] + term
+            return tuple(
+                total + scaled[i] * plain[j] for total, (i, j) in zip(sums, pairs))
+
+        sums = lax.fori_loop(0, cells // 128, add_block, sums)
 
     lane = lax.broadcasted_iota(jnp.int32, (freq, 128), 1)
     packed = jnp.zeros((freq, 128), jnp.float32)

time: 14.8 us -> 14.9 us (level)
  no operation moved by 1% of the time
where the time goes in v2:
time: 14.9 us; the launch traced here: 14.7 us
  Pallas kernels  14.1 us (95%)
  between operations  0.64 us (4%)
    pallas_call x1, Pallas kernels, on_device_kernel(): pl.pallas_call(functools.partial(kernel, space_count, lax.axis_size('var'...  13.2 us
    pallas_call x1, Pallas kernels, on_device_kernel(): pl.pallas_call(functools.partial(modes_kernel, space_count), out_shape=(j...  0.92 us

profile of v2, /device:TPU:1, one launch (start us, length us, event | category | flops | bytes accessed | tf_op | source)
XLA Modules:
  0.0 14.7 jit_solution(9077329200262026832)
XLA Ops:
  0.6 13.2 %shard_map.50 = (f32[6,5,8,512]{3,2,1,0:T(8,128)S(1)}, f32[8,128]{1,0:T(8,128)S(1)}) custom-call(bf16[5,256,512]{2,1,0:T(8,128)(2,1)} %bitcast.3, f32[5,512]{1,0:T(8,128)} %w_hbm.1, s32[32]{0:T(128)} %bins_hbm.1), custom_call_target="tpu_custom_call" | custom-call | tf_op jit(solution)/shard_map/pallas_call | solution.py:237
  13.8 0.9 %shard_map.51 = (f32[6,5,8,512]{3,2,1,0:T(8,128)}, f32[6,8,6]{2,1,0:T(8,128)}) custom-call(f32[6,5,8,512]{3,2,1,0:T(8,128)S(1)} %get-tuple-element.6.values, f32[8,128]{1,0:T(8,128)S(1)} %get-tuple-element.7.gram_ref), custom_call_target="tpu_custom_call" | custom-call | tf_op jit(solution)/shard_map/pallas_call | solution.py:265

commit v3 on v2

--- a/solution.py
+++ b/solution.py
@@ -93,17 +93,19 @@
     basis = basis_rows(bins_ref, frames, seg, var, var_count)
 
     pl.semaphore_wait(barrier, space_count + 1)
-    early = 2
+    early = 1
     copies = [
         pltpu.make_async_remote_copy(
             src_ref=send.at[v], dst_ref=recv.at[v], send_sem=send_sem.at[v], recv_sem=recv_sem.at[v],
             device_id={"seg": other}, device_id_type=MESH)
         for v in range(variables)]
 
-    def transform(v):
+    def transform(v, start=None):
         pltpu.make_async_copy(x_hbm.at[v], x_vmem.at[v], x_sem.at[v]).wait()
         summed = jnp.dot(basis, x_vmem[v], preferred_element_type=jnp.float32)
         send[v] = summed[:2 * rows].astype(send.dtype)
+        if start is not None:
+            start()
         own = summed[2 * rows:3 * rows].astype(jnp.bfloat16).astype(jnp.float32)
         own_half[v] = summed[3 * rows:]
         for part in range(2):
@@ -112,8 +114,7 @@
     @pl.when(var == 0)
     def _():
         for v in range(variables):
-            transform(v)
-            copies[v].start()
+            transform(v, copies[v].start)
         for copy in copies[:early]:
             copy.wait_send()
         pl.semaphore_signal(turn_sem, inc=1, device_id={"var": 1 - var}, device_id_type=MESH)

time: 14.9 us -> 14.9 us (level)
  the two profiles are of different devices: /device:TPU:1 before, /device:TPU:0 now
where the time goes in v3:
time: 14.9 us; the launch traced here: 14.7 us
  Pallas kernels  14.1 us (95%)
  between operations  0.64 us (4%)
    pallas_call x1, Pallas kernels, on_device_kernel(): pl.pallas_call(functools.partial(kernel, space_count, lax.axis_size('var'...  13.2 us
    pallas_call x1, Pallas kernels, on_device_kernel(): pl.pallas_call(functools.partial(modes_kernel, space_count), out_shape=(j...  0.92 us

profile of v3, /device:TPU:0, one launch (start us, length us, event | category | flops | bytes accessed | tf_op | source)
XLA Modules:
  0.0 14.7 jit_solution(18430883458707236039)
XLA Ops:
  0.6 13.2 %shard_map.50 = (f32[6,5,8,512]{3,2,1,0:T(8,128)S(1)}, f32[8,128]{1,0:T(8,128)S(1)}) custom-call(bf16[5,256,512]{2,1,0:T(8,128)(2,1)} %bitcast.3, f32[5,512]{1,0:T(8,128)} %w_hbm.1, s32[32]{0:T(128)} %bins_hbm.1), custom_call_target="tpu_custom_call" | custom-call | tf_op jit(solution)/shard_map/pallas_call | solution.py:238
  13.8 0.9 %shard_map.51 = (f32[6,5,8,512]{3,2,1,0:T(8,128)}, f32[6,8,6]{2,1,0:T(8,128)}) custom-call(f32[6,5,8,512]{3,2,1,0:T(8,128)S(1)} %get-tuple-element.6.values, f32[8,128]{1,0:T(8,128)S(1)} %get-tuple-element.7.gram_ref), custom_call_target="tpu_custom_call" | custom-call | tf_op jit(solution)/shard_map/pallas_call | solution.py:266

commit v4 on v1

--- a/solution.py
+++ b/solution.py
@@ -103,10 +103,12 @@
             device_id={"seg": other}, device_id_type=MESH)
         for v in range(variables)]
 
-    def transform(v):
+    def transform(v, start=None):
         loads[v].wait()
         summed = jnp.dot(basis, x_vmem[v], preferred_element_type=jnp.float32)
         send[v] = summed[:2 * rows].astype(send.dtype)
+        if start is not None:
+            start()
         own = summed[2 * rows:3 * rows].astype(jnp.bfloat16).astype(jnp.float32)
         own_half[v] = summed[3 * rows:]
         for part in range(2):
@@ -115,8 +117,7 @@
     @pl.when(var == 0)
     def _():
         for v in range(variables):
-            transform(v)
-            copies[v].start()
+            transform(v, copies[v].start)
         for copy in copies[:early]:
             copy.wait_send()
         pl.semaphore_signal(turn_sem, inc=1, device_id={"var": 1 - var}, device_id_type=MESH)

time: 14.8 us -> 14.8 us (level)
  no operation moved by 1% of the time
where the time goes in v4:
time: 14.8 us; the launch traced here: 14.7 us
  Pallas kernels  14 us (95%)
  between operations  0.64 us (4%)
    pallas_call x1, Pallas kernels, on_device_kernel(): pl.pallas_call(functools.partial(kernel, space_count, lax.axis_size('var'...  13.1 us
    pallas_call x1, Pallas kernels, on_device_kernel(): pl.pallas_call(functools.partial(modes_kernel, space_count), out_shape=(j...  0.92 us

profile of v4, /device:TPU:1, one launch (start us, length us, event | category | flops | bytes accessed | tf_op | source)
XLA Modules:
  0.0 14.7 jit_solution(4716328132050572296)
XLA Ops:
  0.6 13.1 %shard_map.50 = (f32[6,5,8,512]{3,2,1,0:T(8,128)S(1)}, f32[8,128]{1,0:T(8,128)S(1)}) custom-call(bf16[5,256,512]{2,1,0:T(8,128)(2,1)} %bitcast.3, f32[5,512]{1,0:T(8,128)} %w_hbm.1, s32[32]{0:T(128)} %bins_hbm.1), custom_call_target="tpu_custom_call" | custom-call | tf_op jit(solution)/shard_map/pallas_call | solution.py:241
  13.8 0.9 %shard_map.51 = (f32[6,5,8,512]{3,2,1,0:T(8,128)}, f32[6,8,6]{2,1,0:T(8,128)}) custom-call(f32[6,5,8,512]{3,2,1,0:T(8,128)S(1)} %get-tuple-element.6.values, f32[8,128]{1,0:T(8,128)S(1)} %get-tuple-element.7.gram_ref), custom_call_target="tpu_custom_call" | custom-call | tf_op jit(solution)/shard_map/pallas_call | solution.py:269
